TPU v7x, 512 devices: a whole 4x4x16 slice. The times are simulated.
512 devices in a mesh: dp: 64 (over x, z), sub: 8 (over y, core).
Axes of the slice: x: 4, y: 4, z: 16, core: 2. Of those that a mesh axis runs over, the one named last changes fastest.
Arguments:
- points: bfloat16 [65536, 768], P(('dp', 'sub'))
- cand_rows: int32 [3, 2048], P(None, ('dp', 'sub')), may hold values from 0 to 127
- cand_count: int32 [3, 512], P(None, ('dp', 'sub')), may hold values from 0 to 4, as said below
Outputs:
- weights: float32 [3, 65536], P(None, ('dp', 'sub'))
Inputs may be any that keep to these rules, and one draw needn't show every extreme that they name: `cand_rows`: local row numbers on the device whose slots they fill; slots at or past the count are ignored. `cand_count`: in every round the devices of each group along sub hold exactly 16 candidates together; in every round some device holds 4.
All inputs are finite; a program needn't handle non-finite values.
Results may differ from a plain program's by a relative error of at most 0.0003.
Values may be sent and summed in bfloat16 or wider, within the bound.
A program may use at most 64 MiB of HBM per device.

v0:
```python
import jax
import jax.numpy as jnp
from jax import lax
from jax.experimental import pallas as pl
from jax.experimental.pallas import tpu as pltpu
from jax.sharding import PartitionSpec as P

ROUNDS = 3
SLOTS = 4
XS = 4
ZS = 16
YS = 4
SUBS = 8
RAW = 16
BLK = 8
SHARE = 2
MESH = pl.DeviceIdType.MESH
F32 = jnp.float32
INF = float("inf")


def kernel(
    npts,
    rows_in,
    counts_in,
    points_ref,
    out_ref,
    rows_ref,
    cnt_ref,
    raw,
    slots,
    cand,
    pall,
    mins,
    squares,
    line,
    near,
    zsum,
    xsum,
    local_sem,
    slots_send,
    slots_recv,
    z_block_send,
    x_send,
    z_block_recv,
    x_recv,
    far_send,
    far_z_send,
    far_recv,
    far_z_recv,
    pts_send,
    pts_recv,
    line_send,
    line_recv,
    z_send,
    z_recv,
    c_send,
    c_recv,
):
    dp = lax.axis_index("dp")
    sub = lax.axis_index("sub")
    x, z = lax.div(dp, ZS), lax.rem(dp, ZS)
    y, core = lax.div(sub, 2), lax.rem(sub, 2)
    npd, width = points_ref.shape

    def at_x(d):
        return (lax.rem(x + d, XS) * ZS + z, sub)

    def at_z(d):
        return (x * ZS + lax.rem(z + d, ZS), sub)

    def at_y(d):
        return (dp, lax.rem(y + d, YS) * 2 + core)

    other_core = (dp, y * 2 + (1 - core))
    z_to = {d: at_z(d % ZS) for d in (1, -1, 2, -2, 3, -3, 4, -4)}
    x_to = {d: at_x(d) for d in (1, 2, 3)}
    y_right, y_left = at_y(1), at_y(3)

    own_points = pltpu.make_async_copy(points_ref, raw, local_sem.at[0])
    own_points.start()
    own_rows = pltpu.make_async_copy(rows_in, rows_ref, local_sem.at[1])
    own_rows.start()
    own_counts = pltpu.make_async_copy(counts_in, cnt_ref, local_sem.at[2])
    own_counts.start()
    barrier = pltpu.get_barrier_semaphore()
    far_first = ((2, 0), (2, 1), (1, 0), (3, 0), (1, 1), (3, 1), (0, 1))
    members = [(dp, lax.rem(y + d, YS) * 2 + (1 - core if other else core)) for d, other in far_first]
    partners = [*z_to.values(), *x_to.values(), *members]
    for device in partners:
        pl.semaphore_signal(barrier, inc=1, device_id=device, device_id_type=MESH)

    row = lax.broadcasted_iota(jnp.int32, (RAW, npd), 0)
    lane = lax.broadcasted_iota(jnp.int32, (RAW, npd), 1)
    here = lax.broadcasted_iota(jnp.int32, (npd, npd), 0)
    there = lax.broadcasted_iota(jnp.int32, (npd, npd), 1)
    same_round = (here & (RAW - 1)) == ROUNDS * SLOTS + ((there & (RAW - 1)) >> 2)
    before = jnp.where(same_round & ((here >> 4) < (there >> 4)), 1.0, 0.0)
    itself = jnp.where(same_round & ((here >> 4) == (there >> 4)), 1.0, 0.0)
    slot = lane & (RAW - 1)
    slot_round = jnp.where(slot < ROUNDS * SLOTS, slot >> 2, -1)
    slot_index = (slot & (SLOTS - 1)).astype(F32)
    wanted = (SHARE * sub + (row & 1)).astype(F32)
    wanted_round = slot_round == (row >> 1)
    own_rows.wait()
    own_counts.wait()
    target = jnp.full((RAW, npd), -1, jnp.int32)
    counts = jnp.zeros((RAW, npd), F32)
    for r in range(ROUNDS):
        counts = jnp.where(row == ROUNDS * SLOTS + r, cnt_ref[0, r].astype(F32), counts)
        for i in range(SLOTS):
            target = jnp.where(row == r * SLOTS + i, rows_ref[r, i], target)
    pick = jnp.where(lane == target, 1.0, 0.0).astype(jnp.bfloat16)
    own_points.wait()
    mine = raw[...]
    block = jnp.dot(pick, mine, preferred_element_type=F32)
    slots[sub, :, :npd] = (block[:, :npd] + counts).astype(jnp.bfloat16)
    slots[sub, :, npd:] = block[:, npd:].astype(jnp.bfloat16)

    pl.semaphore_wait(barrier, len(partners))

    def remote(src, dst, send, recv, device):
        return pltpu.make_async_remote_copy(
            src_ref=src, dst_ref=dst, send_sem=send, recv_sem=recv, device_id=device, device_id_type=MESH
        )

    def to_sides(place, count, group):
        for d, column in ((1, 2), (3, 3)):
            src, dst = cand.at[0, pl.ds(place, count)], cand.at[column, pl.ds(place, count)]
            remote(src, dst, x_send, x_recv.at[group], x_to[d]).start()

    def to_far(place):
        remote(cand.at[0, place], cand.at[1, place], far_send, far_recv.at[place - 12], x_to[2]).start()

    def far_along_z(src, place, count, group, d, lanes=None):
        src, dst = cand.at[1, pl.ds(src, count)], cand.at[1, pl.ds(place, count)]
        if lanes is not None:
            part = pl.ds(lanes * (width // 2), width // 2)
            src, dst = src.at[:, :, part], dst.at[:, :, part]
        remote(src, dst, far_z_send, far_z_recv.at[group], z_to[d]).start()

    def along_z(src, place, d, lanes=None):
        if lanes is None:
            src, dst = cand.at[0, src], cand.at[0, place]
        else:
            part = pl.ds(lanes * (width // 2), width // 2)
            src, dst = cand.at[0, src, :, part], cand.at[0, place, :, part]
        remote(src, dst, z_block_send, z_block_recv.at[place + (lanes or 0)], z_to[d]).start()

    def z_arrived(*places):
        for place in places:
            wait_bytes(cand.at[0, place], z_block_recv.at[place])

    def wait_bytes(ref, sem):
        pltpu.make_async_copy(ref, ref, sem).wait()

    for device in members:
        remote(slots.at[sub], slots.at[sub], slots_send, slots_recv, device).start()
    pall[sub] = mine.T
    wait_bytes(slots.at[pl.ds(0, SUBS - 1)], slots_recv)
    flat = slots[...].reshape(SUBS * RAW, width)
    known = flat[:, :npd].astype(F32)
    offset = jnp.sum(known * before, axis=0, keepdims=True)
    count = jnp.sum(known * itself, axis=0, keepdims=True)
    choice = wanted_round & (slot_index < count) & (offset + slot_index == wanted)
    share = jnp.dot(jnp.where(choice, 1.0, 0.0).astype(jnp.bfloat16), flat, preferred_element_type=F32)
    cand[0, 13] = share[:BLK].astype(jnp.bfloat16)

    along_z(13, 12, 4)
    along_z(13, 14, -4)
    to_far(13)
    for place, d in ((1, 2), (2, -2), (5, 1), (9, -1)):
        along_z(13, place, d)
    to_sides(13, 1, 3)

    slot_right, slot_left, slot_far = (lax.rem(y + d, YS) * 2 + core for d in (1, 3, 2))
    top, low = pl.ds(0, width // 2), pl.ds(width // 2, width // 2)
    mine_at = pall.at[sub]
    pts_right = remote(mine_at, mine_at, pts_send.at[0], pts_recv.at[0], y_right)
    pts_left = remote(mine_at, mine_at, pts_send.at[1], pts_recv.at[1], y_left)
    pts_core = remote(mine_at, mine_at, pts_send.at[2], pts_recv.at[2], other_core)
    pts_right.start()
    pts_left.start()
    pts_core.start()

    z_arrived(12)
    to_far(12)
    along_z(12, 15, 4, 0)
    for place, d in ((7, 3), (0, 2), (4, 1), (8, -1)):
        along_z(12, place, d)
    z_arrived(14)
    to_far(14)
    along_z(14, 15, -4, 1)
    for place, d in ((11, -3), (3, -2), (10, -1), (6, 1)):
        along_z(14, place, d)
    to_sides(12, 1, 3)
    to_sides(14, 1, 3)

    pts_right.wait_recv()
    near_left = pall.at[slot_left]
    far_top = remote(near_left.at[top], near_left.at[top], pts_send.at[3], pts_recv.at[3], y_right)
    core_left = remote(near_left, near_left, pts_send.at[4], pts_recv.at[4], other_core)
    far_top.start()
    core_left.start()
    pts_left.wait_recv()
    near_right = pall.at[slot_right]
    far_low = remote(near_right.at[low], near_right.at[low], pts_send.at[5], pts_recv.at[5], y_left)
    core_right = remote(near_right, near_right, pts_send.at[6], pts_recv.at[6], other_core)
    far_low.start()
    core_right.start()
    for place in (12, 13, 14):
        wait_bytes(cand.at[1, place], far_recv.at[place - 12])
    far_along_z(12, 15, 1, 3, 4, 0)
    far_along_z(14, 15, 1, 3, -4, 1)
    far_along_z(12, 7, 1, 1, 3)
    far_along_z(14, 11, 1, 2, -3)
    far_along_z(12, 0, 2, 0, 2)
    far_along_z(13, 2, 2, 0, -2)
    far_along_z(12, 4, 3, 1, 1)
    far_along_z(12, 8, 3, 2, -1)

    for group in range(3):
        z_arrived(*range(4 * group, 4 * group + 4))
        to_sides(4 * group, 4, group)
    half_block = cand.at[0, 15, :, pl.ds(0, width // 2)]
    wait_bytes(half_block, z_block_recv.at[15])
    wait_bytes(half_block, z_block_recv.at[16])
    to_sides(15, 1, 3)

    far_top.wait_recv()
    far_low.wait_recv()
    far = pall.at[slot_far]
    core_far = remote(far, far, pts_send.at[7], pts_recv.at[7], other_core)
    core_far.start()

    def absorb(first, count):
        for group in range(first, first + count):
            wait_bytes(cand.at[pl.ds(2, 2), pl.ds(0, 4)], x_recv.at[group])
            wait_bytes(cand.at[1, pl.ds(0, 4 if group < 3 else 1)], far_z_recv.at[group])
        blocks = XS * 4 * count
        rows = cand[:, 4 * first : 4 * (first + count)].reshape(blocks, BLK, width)
        half = jnp.zeros((blocks, BLK, npd), F32)
        for t in range(width // npd):
            piece = rows[:, :, t * npd : (t + 1) * npd].astype(F32)
            half = half + piece * piece
        half = 0.5 * jnp.sum(half, axis=2, keepdims=True)
        flat = rows.reshape(blocks * BLK, width)
        for j in range(SUBS // 2):
            group = jnp.concatenate([pall[2 * j], pall[2 * j + 1]], axis=1)
            dots = jnp.dot(flat, group, preferred_element_type=F32)
            best = jnp.min(half - dots.reshape(blocks, BLK, 2 * npd), axis=0)
            mins[j] = best if first == 0 else jnp.minimum(mins[j], best)

    pts_core.wait_recv()
    core_left.wait_recv()
    core_right.wait_recv()
    core_far.wait_recv()
    absorb(0, 3)
    for b in range(SUBS):
        wide = pall[b].astype(F32)
        squares[b : b + 1, :] = jnp.sum(wide * wide, axis=0, keepdims=True)
    absorb(3, 1)

    for j in range(SUBS // 2):
        for r in range(ROUNDS):
            low_r = jnp.min(mins[j, r * SHARE : (r + 1) * SHARE, :], axis=0, keepdims=True)
            for h in range(2):
                line[sub, r, 2 * j + h : 2 * j + h + 1, :] = low_r[:, h * npd : (h + 1) * npd]

    for device in members:
        remote(line.at[sub], line.at[sub], line_send, line_recv, device).start()
    wait_bytes(line.at[pl.ds(0, SUBS - 1)], line_recv)

    lanes = lax.broadcasted_iota(jnp.int32, (1, npd), 1)
    least = None
    total = jnp.zeros((1, npd), F32)
    for r in range(ROUNDS):
        now = jnp.min(line[:, r], axis=0)
        least = now if least is None else jnp.minimum(least, now)
        dist = jnp.maximum(squares[...] + 2.0 * least, 0.0)
        near[r] = dist
        part = jnp.sum(jnp.sum(dist, axis=0, keepdims=True), axis=1, keepdims=True)
        total = jnp.where(lanes == r, part, total)

    zsum[0] = total

    for d in (8, 7, 9, 6, 10, 5, 11, 4, 12, 3, 13, 2, 14, 1, 15):
        remote(zsum.at[0], zsum.at[ZS - d], z_send, z_recv, at_z(d)).start()
    wait_bytes(zsum.at[pl.ds(0, ZS - 1)], z_recv)
    xsum[0] = jnp.sum(zsum[...], axis=0)
    for d in (1, 3, 2):
        remote(xsum.at[0], xsum.at[XS - d], c_send, c_recv, x_to[d]).start()
    wait_bytes(xsum.at[pl.ds(0, XS - 1)], c_recv)
    cost = jnp.sum(xsum[...], axis=0)
    for r in range(ROUNDS):
        cost_r = jnp.sum(jnp.where(lanes == r, cost, 0.0), axis=1, keepdims=True)
        out_ref[r : r + 1, :] = npts * near[r, pl.ds(sub, 1), :] / cost_r

    wait_bytes(slots.at[pl.ds(0, SUBS - 1)], slots_send)
    wait_bytes(cand.at[0, pl.ds(0, 15)], z_block_send)
    wait_bytes(cand.at[pl.ds(0, 2)], x_send)
    wait_bytes(cand.at[0, pl.ds(0, 3)], far_send)
    wait_bytes(cand.at[0, pl.ds(0, 13)], far_z_send)
    for copy in (pts_right, pts_left, pts_core, far_top, core_left, far_low, core_right, core_far):
        copy.wait_send()
    wait_bytes(line.at[pl.ds(0, SUBS - 1)], line_send)
    wait_bytes(zsum.at[pl.ds(0, ZS - 1)], z_send)
    wait_bytes(xsum.at[pl.ds(0, XS - 1)], c_send)


def shards(points, cand_rows, cand_count):
    npd, width = points.shape
    npts = float(npd * lax.axis_size(("dp", "sub")))
    dma = pltpu.SemaphoreType.DMA
    operands = (cand_rows, cand_count.reshape(1, ROUNDS), points)
    return pl.pallas_call(
        lambda *refs: kernel(npts, *refs),
        out_shape=jax.ShapeDtypeStruct((ROUNDS, npd), F32),
        in_specs=[
            pl.BlockSpec(memory_space=pl.ANY),
            pl.BlockSpec(memory_space=pl.ANY),
            pl.BlockSpec(memory_space=pl.ANY),
        ],
        out_specs=pl.BlockSpec(memory_space=pltpu.VMEM),
        scratch_shapes=[
            pltpu.SMEM((ROUNDS, SLOTS), jnp.int32),
            pltpu.SMEM((1, ROUNDS), jnp.int32),
            pltpu.VMEM((npd, width), jnp.bfloat16),
            pltpu.VMEM((SUBS, RAW, width), jnp.bfloat16),
            pltpu.VMEM((XS, ZS, BLK, width), jnp.bfloat16),
            pltpu.VMEM((SUBS, width, npd), jnp.bfloat16),
            pltpu.VMEM((SUBS // 2, BLK, 2 * npd), F32),
            pltpu.VMEM((SUBS, npd), F32),
            pltpu.VMEM((SUBS, ROUNDS, SUBS, npd), F32),
            pltpu.VMEM((ROUNDS, SUBS, npd), F32),
            pltpu.VMEM((ZS, 1, npd), F32),
            pltpu.VMEM((XS, 1, npd), F32),
            dma((3,)),
            dma,
            dma,
            dma,
            dma,
            dma((17,)),
            dma((4,)),
            dma,
            dma,
            dma((3,)),
            dma((4,)),
            dma((8,)),
            dma((8,)),
            dma,
            dma,
            dma,
            dma,
            dma,
            dma,
        ],
        compiler_params=pltpu.CompilerParams(
            collective_id=0, has_side_effects=True, vmem_limit_bytes=40 * 1024 * 1024
        ),
        cost_estimate=pl.CostEstimate(
            flops=2 * 1024 * 1024 * width, bytes_accessed=npd * width * 2, transcendentals=0
        ),
    )(*(pltpu.with_memory_space_constraint(value, pltpu.HBM) for value in operands))


def solution(mesh):
    in_specs = (P(("dp", "sub"), None), P(None, ("dp", "sub")), P(None, ("dp", "sub")))
    out_specs = P(None, ("dp", "sub"))
    return jax.shard_map(shards, mesh=mesh, in_specs=in_specs, out_specs=out_specs, check_vma=False)
```

profile of v0, /device:TPU:1, one launch (start us, length us, event | category | flops | bytes accessed | tf_op | source)
XLA Modules:
  0.0 47.3 jit_solution(3735033743032636257)
XLA Ops:
  0.0 46.7 %shard_map.37 = f32[3,128]{1,0:T(4,128)S(1)} custom-call(s32[3,4]{1,0:T(4,128)} %refs_0_.1, s32[1,3]{1,0:T(1,128)} %bitcast.1, bf16[128,768]{1,0:T(8,128)(2,1)} %refs_2_.1), custom_call_target="tpu_custom_call" | custom-call | flops 1610612736 | bytes 196608 | tf_op jit(solution)/shard_map/pallas_call | solution.py:316
  46.7 0.6 %copy.5 = f32[3,128]{1,0:T(4,128)} copy(f32[3,128]{1,0:T(4,128)S(1)} %shard_map.37) | data formatting | bytes 3072
where the time goes:
time: 47.5 us; the launch traced here: 47.3 us
  Pallas kernels  46.7 us (98%)
  local copies, waits for them, and re-layouts  0.58 us (1%)
    pallas_call x1, Pallas kernels, shards(): pl.pallas_call(lambda *refs: kernel(npts, *refs), out_shape=jax.ShapeDtyp...  46.7 us

commit v1 on v0

--- a/solution.py
+++ b/solution.py
@@ -255,11 +255,10 @@
     core_left.wait_recv()
     core_right.wait_recv()
     core_far.wait_recv()
-    absorb(0, 3)
     for b in range(SUBS):
         wide = pall[b].astype(F32)
         squares[b : b + 1, :] = jnp.sum(wide * wide, axis=0, keepdims=True)
-    absorb(3, 1)
+    absorb(0, 4)
 
     for j in range(SUBS // 2):
         for r in range(ROUNDS):

time: 47.5 us -> 47.2 us (level)
  no operation moved by 1% of the time
where the time goes in v1:
time: 47.2 us; the launch traced here: 47.1 us
  Pallas kernels  46.5 us (99%)
  local copies, waits for them, and re-layouts  0.58 us (1%)
    pallas_call x1, Pallas kernels, shards(): pl.pallas_call(lambda *refs: kernel(npts, *refs), out_shape=jax.ShapeDtyp...  46.5 us

profile of v1, /device:TPU:1, one launch (start us, length us, event | category | flops | bytes accessed | tf_op | source)
XLA Modules:
  0.0 47.1 jit_solution(8901338186731710203)
XLA Ops:
  0.0 46.5 %shard_map.37 = f32[3,128]{1,0:T(4,128)S(1)} custom-call(s32[3,4]{1,0:T(4,128)} %refs_0_.1, s32[1,3]{1,0:T(1,128)} %bitcast.1, bf16[128,768]{1,0:T(8,128)(2,1)} %refs_2_.1), custom_call_target="tpu_custom_call" | custom-call | flops 1610612736 | bytes 196608 | tf_op jit(solution)/shard_map/pallas_call | solution.py:315
  46.5 0.6 %copy.5 = f32[3,128]{1,0:T(4,128)} copy(f32[3,128]{1,0:T(4,128)S(1)} %shard_map.37) | data formatting | bytes 3072
